TPU v7x, 128 devices: a whole 4x4x4 slice. The times are simulated.
128 devices in a mesh: seq: 4 (over z), head: 32 (over y, x, core).
Axes of the slice: x: 4, y: 4, z: 4, core: 2. Of those that a mesh axis runs over, the one named last changes fastest.
Arguments:
- queries: float32 [8192, 4096], P('seq', 'head'), may hold values from -6 to 6
- key_rows: float32 [8192, 4096], P('seq', 'head'), may hold values from -6 to 6
- values: float32 [8192, 4096], P('seq', 'head'), may hold values from -6 to 6
- out_weight: bfloat16 [4096, 2048], P('head'), may hold values from -0.09375 to 0.09375
- expert_ids: int32 [8192, 8], P(('seq', 'head')), may hold values from 0 to 127, all different within a row; in each aligned block of 64 rows (0 to 63, 64 to 127, ...) at most 8 rows name the same one
- gate_ints: int32 [8192, 8], P(('seq', 'head')), may hold values from 1 to 1023
- w_gate: bfloat16 [128, 2048, 768], P(('seq', 'head')), may hold values from -0.125 to 0.125
- w_up: bfloat16 [128, 2048, 768], P(('seq', 'head')), may hold values from -0.125 to 0.125
- w_down: bfloat16 [128, 768, 2048], P(('seq', 'head')), may hold values from -0.21875 to 0.21875
Outputs:
- layer_out: float32 [8192, 2048], P(('seq', 'head'))
Inputs may be any that keep to these rules, and one draw needn't show every extreme that they name: `expert_ids`: each row names 8 different experts. Within the rows of one device (aligned blocks of 64 rows) no expert is named more than 8 times, a bound that some block reaches.
All inputs are finite; a program needn't handle non-finite values.
Results may differ from a plain program's by a relative error of at most 0.017.
Values may be sent and summed in bfloat16 or wider, within the bound.
A program may use at most 128 MiB of HBM per device.

v0:
```python
import math
import jax
import jax.numpy as jnp
from jax import lax
from jax.sharding import PartitionSpec as P

DH = 128
HIGH = lax.Precision.HIGHEST


def cut_along(array, dim, devices):
    dims = array.shape
    blocks = array.reshape(*dims[:dim], devices, dims[dim] // devices, *dims[dim + 1 :])
    return jnp.moveaxis(blocks, dim, 0)


def laid_out(blocks, dim):
    blocks = jnp.moveaxis(blocks, 0, dim)
    dims = blocks.shape
    return blocks.reshape(*dims[:dim], dims[dim] * dims[dim + 1], *dims[dim + 2 :])


def exchange_both(array, axis, axes, splits, concats):
    sizes = [lax.axis_size(a) for a in axes]
    blocks = cut_along(array, splits[0], sizes[0])
    blocks = jnp.moveaxis(cut_along(blocks, splits[1] + 1, sizes[1]), 0, 1)
    inside = blocks.shape[2:]
    blocks = blocks.reshape(-1, *inside)
    blocks = lax.all_to_all(blocks, axis, split_axis=0, concat_axis=0, tiled=True)
    blocks = laid_out(blocks.reshape(*sizes, *inside), concats[0] + 1)
    return laid_out(blocks, concats[1])


def causal_linear(query_heads, key_heads, value_heads):
    heads, length, width = query_heads.shape
    block = math.gcd(512, length)
    count = length // block

    def split(array):
        return array.reshape(heads, count, block, width).transpose(1, 0, 2, 3)

    lower = jnp.tril(jnp.ones((block, block), jnp.float32))

    def advance(state, inputs):
        query_block, key_block, value_block = inputs
        scores = jnp.einsum("hid,hjd->hij", query_block, key_block, precision=HIGH) * lower
        output = jnp.einsum("hij,hjd->hid", scores, value_block, precision=HIGH)
        output = output + jnp.einsum("hid,hde->hie", query_block, state, precision=HIGH)
        state = state + jnp.einsum("hjd,hje->hde", key_block, value_block, precision=HIGH)
        return (state, output)

    start = jnp.zeros((heads, width, width), jnp.float32)
    state, outputs = lax.scan(
        advance, start, (split(query_heads), split(key_heads), split(value_heads))
    )
    return (outputs.transpose(1, 0, 2, 3).reshape(heads, length, width), state)


def shards(queries, key_rows, values, out_weight, expert_ids, gate_ints, w_gate, w_up, w_down):
    length = queries.shape[0]
    heads_here = queries.shape[1] // DH

    def split_heads(array):
        return array.reshape(length, heads_here, DH).transpose(1, 0, 2)

    query_heads = split_heads(queries)
    local_out, local_state = causal_linear(query_heads, split_heads(key_rows), split_heads(values))
    every_state = lax.all_gather(
        local_state[None].astype(jnp.bfloat16), "seq", axis=0, tiled=True
    ).astype(jnp.float32)
    before = (jnp.arange(every_state.shape[0], dtype=jnp.int32) < lax.axis_index("seq")).astype(
        jnp.float32
    )
    earlier = jnp.sum(every_state * before[:, None, None, None], axis=0)
    heads_out = local_out + jnp.einsum("hid,hde->hie", query_heads, earlier, precision=HIGH)
    heads_out = heads_out * lax.rsqrt(
        jnp.mean(heads_out * heads_out, axis=-1, keepdims=True) + 1e-06
    )
    attn = heads_out.transpose(1, 0, 2).reshape(length, heads_here * DH).astype(jnp.bfloat16)
    head_count = lax.axis_size("head")
    seq_count = lax.axis_size("seq")
    tok_count = length // head_count
    all_heads = lax.all_to_all(attn, "head", split_axis=0, concat_axis=1, tiled=True)
    all_rows = lax.all_gather(out_weight, "head", axis=0, tiled=True)
    projected = jnp.dot(all_heads, all_rows, preferred_element_type=jnp.float32)
    normed = (
        projected * lax.rsqrt(jnp.mean(projected * projected, axis=-1, keepdims=True) + 1e-06)
    ).astype(jnp.bfloat16)
    gates = gate_ints.astype(jnp.float32)
    gates = gates / jnp.sum(gates, axis=-1, keepdims=True)
    top_count = expert_ids.shape[1]
    local_experts = w_gate.shape[0]
    devices = seq_count * head_count
    experts = local_experts * devices
    capacity = max(2, 2 * tok_count * top_count // experts)
    width = normed.shape[1]
    flat_ids = expert_ids.reshape(-1)
    assigned = flat_ids.shape[0]
    onehot = (flat_ids[:, None] == jnp.arange(experts, dtype=jnp.int32)[None, :]).astype(jnp.int32)
    before_count = jnp.cumsum(onehot, axis=0, dtype=jnp.int32) - onehot
    position = jnp.sum(before_count * onehot, axis=1, dtype=jnp.int32)
    slot_index = flat_ids * capacity + position
    source = (
        jnp.zeros((experts * capacity,), jnp.int32)
        .at[slot_index]
        .set(jnp.arange(assigned, dtype=jnp.int32))
    )
    filled = jnp.zeros((experts * capacity,), jnp.bool_).at[slot_index].set(True)
    picked = normed[source // top_count]
    outgoing = jnp.where(filled[:, None], picked, jnp.zeros_like(picked))
    outgoing = outgoing.reshape(seq_count, head_count, local_experts, capacity, width)
    received = exchange_both(outgoing, ("seq", "head"), ("seq", "head"), (0, 1), (0, 1))
    expert_received = received.reshape(devices, local_experts, capacity, width)
    gate_val = jnp.einsum(
        "nesd,edf->nesf", expert_received, w_gate, preferred_element_type=jnp.float32
    )
    up_val = jnp.einsum("nesd,edf->nesf", expert_received, w_up, preferred_element_type=jnp.float32)
    act = (jax.nn.silu(gate_val) * up_val).astype(jnp.bfloat16)
    result = jnp.einsum("nesf,efd->nesd", act, w_down, preferred_element_type=jnp.float32).astype(
        jnp.bfloat16
    )
    result = result.reshape(seq_count, head_count, local_experts, capacity, width)
    returned = exchange_both(result, ("seq", "head"), ("seq", "head"), (0, 1), (0, 1))
    returned = returned.reshape(experts * capacity, width)
    gathered = returned[slot_index].astype(jnp.float32) * gates.reshape(-1)[:, None]
    mixture = jnp.sum(gathered.reshape(tok_count, top_count, width), axis=1)
    return projected + mixture


def solution(mesh):
    placed = (
        P("seq", "head"),
        P("seq", "head"),
        P("seq", "head"),
        P("head", None),
        P(("seq", "head"), None),
        P(("seq", "head"), None),
        P(("seq", "head"), None, None),
        P(("seq", "head"), None, None),
        P(("seq", "head"), None, None),
    )
    return jax.shard_map(
        shards, mesh=mesh, in_specs=placed, out_specs=P(("seq", "head"), None), check_vma=False
    )
```

profile of v0, /device:TPU:1, one launch (start us, length us, event | category | flops | bytes accessed | tf_op | source)
XLA Modules:
  0.0 276.8 jit_solution(5523111241887061232)
XLA Ops:
  7.3 30.9 %while.13 = (s32[]{:T(128)}, f32[1,128,128]{2,1,0:T(8,128)S(1)}, f32[4,1,512,128]{3,2,1,0:T(8,128)}, f32[4,1,512,128]{3,2,1,0:T(8,128)}, f32[4,1,512,128]{3,2,1,...) while((s32[]{:T(128)}, f32[1,128,128]{2,1,0:T(8,128)S(1)}, ...), condition=%wide.region_1.2_spmd.clone, body=%wide.region_0.1_spmd.clone.sunk | while | flops 1007534080 | bytes 4656736 | solution.py:53
  7.3 2.2 convolution_multiply_fusion.2
  11.5 2.0 fusion.90
  15.1 2.0 convolution_multiply_fusion.2
  19.1 2.0 fusion.90
  22.8 2.1 convolution_multiply_fusion.2
  24.8 1.9 fusion.89
  26.8 2.0 fusion.90
  30.5 2.0 convolution_multiply_fusion.2
  34.5 2.0 fusion.90
  38.2 2.6 copy.37
  40.8 12.0 %all-gather = bf16[4,128,128]{2,1,0:T(8,128)(2,1)S(1)} all-gather(bf16[1,128,128]{2,1,0:T(8,128)(2,1)S(1)} %convert_element_type.66), channel_id=2, replica_groups=mesh['seq'=4,'head'=32] {'seq'}, dimensions={0}, use_global_device_ids=true | all-gather | bytes 163840 | tf_op jit(solution)/shard_map/all_gather | solution.py:68
  52.8 2.7 multiply_reduce_fusion
  56.5 2.1 copy.26
  58.6 9.8 %all-to-all-start = ((bf16[32,64,128]{2,1,0:T(8,128)(2,1)}), bf16[32,64,128]{2,1,0:T(8,128)(2,1)}, u32[]{:S(2)}, u32[]{:S(2)}) async-start(bf16[32,64,128]{2,1,0:T(8,128)(2,1)} %bitcast.182), calls=%async_computation | async-start | bytes 1048576 | tf_op jit(solution)/shard_map/all_to_all | solution.py:83
  69.5 2.4 scatter_custom_fusion.1
  71.9 2.6 scatter_custom_fusion
  74.7 9.7 %all-to-all-done = bf16[32,64,128]{2,1,0:T(8,128)(2,1)} async-done(((bf16[32,64,128]{2,1,0:T(8,128)(2,1)}), bf16[32,64,128]{2,1,0:T(8,128)(2,1)}, u32[]{:S(2)}, u32[]{:S(2)}) %all-to-all-start) | async-done | bytes 524320 | tf_op jit(solution)/shard_map/all_to_all | solution.py:83
  84.4 6.9 %all-gather.3.cloned.1.call-done = bf16[4096,2048]{1,0:T(8,128)(2,1)} async-done(((bf16[128,2048]{1,0:T(8,128)(2,1)}), bf16[4096,2048]{1,0:T(8,128)(2,1)}) %all-gather.3.cloned.1.call-update) | async-done | bytes 16777232 | tf_op jit(solution)/shard_map/all_gather | solution.py:84
  91.3 9.1 %multiply_reduce_fusion.1 = (f32[64]{0:T(128)S(1)}, f32[64,2048]{1,0:T(8,128)S(1)}) fusion(bf16[4096,2048]{1,0:T(8,128)(2,1)} %all-gather.3.cloned.1.call-done, bf16[32,64,128]{2,1,0:T(8,128)(2,1)} %all-to-all-done), kind=kOutput, calls=%fused_computation.59 | convolution fusion | flops 1074003968 | bytes 17826048 | tf_op jit(solution)/shard_map/dot_general | solution.py:85
  101.2 6.0 %gather_fusion = bf16[1024,2048]{1,0:T(8,128)(2,1)} fusion(bf16[64,2048]{1,0:T(8,128)(2,1)S(1)} %multiply_convert_fusion.1, s32[1024]{0:T(1024)S(1)} %fusion.55), kind=kCustom, calls=%fused_computation | custom fusion | bytes 8392704 | tf_op jit(solution)/shard_map/gather | solution.py:109
  107.3 2.5 bitcast_select_fusion
  109.8 60.2 %all_to_all.26 = bf16[128,1,1,1,8,2048]{5,4,3,2,1,0:T(8,128)(2,1)S(1)} all-to-all(bf16[128,1,1,1,8,2048]{5,4,3,2,1,0:T(8,128)(2,1)S(1)} %bitcast_select_fusion), channel_id=1, replica_groups=mesh['seq'=4,'head'=32] {'seq','head'}, dimensions={0} | all-to-all | bytes 8388608 | tf_op jit(solution)/shard_map/all_to_all | solution.py:29
  170.0 2.3 copy.34
  172.3 2.0 copy-done.2
  174.3 5.2 %fusion.30 = f32[128,8,768]{2,0,1:T(8,128)} fusion(bf16[128,8,2048]{2,0,1:T(8,128)(2,1)S(1)} %bitcast.180, bf16[1,2048,768]{2,1,0:T(8,128)(2,1)S(1)} %copy-done.5), kind=kOutput, calls=%fused_computation.41 | convolution fusion | flops 3221225472 | bytes 10485760 | tf_op jit(solution)/shard_map/nesd,edf->nesf/dot_general | solution.py:117
  179.5 12.3 %convert_bitcast_fusion = bf16[128,1,1,1,8,2048]{5,0,4,3,2,1:T(8,128)(2,1)} fusion(bf16[1,768,2048]{2,1,0:T(8,128)(2,1)S(1)} %copy-done, f32[128,8,768]{2,0,1:T(8,128)} %fusion.30, bf16[128,8,2048]{2,0,1:T(8,128)(2,1)} %bitcast.181, bf16[1,2048,768]{2,1,0:T(8,128)(2,1)} %param.17), kind=kOutput, calls=%fused_computation.37 | convolution fusion | flops 6449266688 | bytes 17825792 | tf_op jit(solution)/shard_map/nesf,efd->nesd/dot_general | solution.py:119
  191.8 6.5 %copy.35 = bf16[128,1,1,1,8,2048]{5,4,3,2,1,0:T(8,128)(2,1)} copy(bf16[128,1,1,1,8,2048]{5,0,4,3,2,1:T(8,128)(2,1)} %convert_bitcast_fusion) | data formatting | bytes 8388608 | tf_op jit(solution)/shard_map/reshape;transpose;transpose;reshape;reshape;reshape | solution.py:28
  198.3 5.6 %all-to-all-start.2 = ((bf16[128,1,1,1,8,2048]{5,4,3,2,1,0:T(8,128)(2,1)}), bf16[128,1,1,1,8,2048]{5,4,3,2,1,0:T(8,128)(2,1)}, u32[]{:S(2)}, u32[]{:S(2)}) async-start(bf16[128,1,1,1,8,2048]{5,4,3,2,1,0:T(8,128)(2,1)} %copy.35), calls=%async_computation.2 | async-start | bytes 8388608 | tf_op jit(solution)/shard_map/all_to_all | solution.py:29
  204.0 52.6 %all-to-all-done.2 = bf16[128,1,1,1,8,2048]{5,4,3,2,1,0:T(8,128)(2,1)} async-done(((bf16[128,1,1,1,8,2048]{5,4,3,2,1,0:T(8,128)(2,1)}), bf16[128,1,1,1,8,2048]{5,4,3,2,1,0:T(8,128)(2,1)}, u32[]{:S(2)}, u32[]{:S(2)}) %all-to-all-start.2) | async-done | bytes 4194336 | tf_op jit(solution)/shard_map/all_to_all | solution.py:29
  256.6 8.0 %gather_fusion.1 = bf16[512,2048]{1,0:T(8,128)(2,1)} fusion(bf16[1024,2048]{1,0:T(8,128)(2,1)} %bitcast.46, s32[1024]{0:T(1024)S(1)} %pad_clamp_fusion), kind=kCustom, calls=%fused_computation.1 | custom fusion | bytes 4196352 | tf_op jit(solution)/shard_map/gather | solution.py:125
  264.6 3.4 %fusion.27 = f32[64,2048]{1,0:T(8,128)S(1)} fusion(bf16[512,2048]{1,0:T(8,128)(2,1)} %gather_fusion.1, f32[64,8]{1,0:T(8,128)S(1)} %copy.36), kind=kLoop, calls=%fused_computation.35 | loop fusion | flops 3014656 | bytes 2623488 | tf_op jit(solution)/shard_map/reduce_sum | solution.py:126
  (54 shorter events, 18.2 us)
Async XLA Ops:
  6.5 172.9 %copy-start = (bf16[1,768,2048]{2,1,0:T(8,128)(2,1)S(1)}, bf16[1,768,2048]{2,1,0:T(8,128)(2,1)}, u32[]{:S(2)}) copy-start(bf16[1,768,2048]{2,1,0:T(8,128)(2,1)} %param.19) | copy-start | bytes 9437188
  6.5 84.7 %all-gather.3.cloned.1.call-start = ((), (), s32[]{:S(2)}) async-start(), calls=%async_computation.3 | async-start | bytes 17301504 | tf_op jit(solution)/shard_map/all_gather | solution.py:84
  52.8 15.5 %copy-start.3 = (s32[64,8]{0,1:T(8,128)S(1)}, s32[64,8]{0,1:T(8,128)}, u32[]{:S(2)}) copy-start(s32[64,8]{0,1:T(8,128)} %param.15) | copy-start | bytes 6148
  58.6 25.8 %all-to-all-start = ((bf16[32,64,128]{2,1,0:T(8,128)(2,1)}), bf16[32,64,128]{2,1,0:T(8,128)(2,1)}, u32[]{:S(2)}, u32[]{:S(2)}) async-start(bf16[32,64,128]{2,1,0:T(8,128)(2,1)} %bitcast.182), calls=%async_computation | async-start | bytes 1048576 | tf_op jit(solution)/shard_map/all_to_all | solution.py:83
  100.3 0.8 copy-start.1
  170.0 4.3 %copy-start.5 = (bf16[1,2048,768]{2,1,0:T(8,128)(2,1)S(1)}, bf16[1,2048,768]{2,1,0:T(8,128)(2,1)}, u32[]{:S(2)}) copy-start(bf16[1,2048,768]{2,1,0:T(8,128)(2,1)} %param.18) | copy-start | bytes 9437188
  172.3 2.0 copy-start.2
  198.2 5.6 %copy-start.4 = (s32[64,8]{0,1:T(8,128)S(1)}, s32[64,8]{0,1:T(8,128)}, u32[]{:S(2)}) copy-start(s32[64,8]{0,1:T(8,128)} %param.16) | copy-start | bytes 6148
  198.3 58.4 %all-to-all-start.2 = ((bf16[128,1,1,1,8,2048]{5,4,3,2,1,0:T(8,128)(2,1)}), bf16[128,1,1,1,8,2048]{5,4,3,2,1,0:T(8,128)(2,1)}, u32[]{:S(2)}, u32[]{:S(2)}) async-start(bf16[128,1,1,1,8,2048]{5,4,3,2,1,0:T(8,128)(2,1)} %copy.35), calls=%async_computation.2 | async-start | bytes 8388608 | tf_op jit(solution)/shard_map/all_to_all | solution.py:29
Sparse Core Ops, SparseCore 0:
  9.6 81.5 all-gather.2
where the time goes:
time: 278 us; the launch traced here: 277 us
  blocking collectives  72.2 us (26%)
  waiting for transfers between devices  69.9 us (25%)
  matrix products  60 us (22%)
  local copies, waits for them, and re-layouts  36.1 us (13%)
  starting transfers between devices  15.4 us (6%)
  between operations  13.6 us (5%)
  other arithmetic  9.54 us (3%)
    all_to_all x1, blocking collectives, exchange_both(): lax.all_to_all(blocks, axis, split_axis=0, concat_axis=0, tiled=True)  60.2 us
    all_to_all x1, waiting for transfers between devices, exchange_both(): lax.all_to_all(blocks, axis, split_axis=0, concat_axis=0, tiled=True)  52.6 us
    dot_general x1, matrix products, shards(): jnp.einsum('nesf,efd->nesd', act, w_down, preferred_element_type=jnp.floa...  12.3 us
    all_gather x1, blocking collectives, shards(): lax.all_gather(local_state[None].astype(jnp.bfloat16), 'seq', axis=0, til...  12 us
    all_to_all x1, starting transfers between devices, shards(): lax.all_to_all(attn, 'head', split_axis=0, concat_axis=1, tiled=True)  9.76 us
    all_to_all x1, waiting for transfers between devices, shards(): lax.all_to_all(attn, 'head', split_axis=0, concat_axis=1, tiled=True)  9.66 us
    dot_general x1, matrix products, shards(): projected = jnp.dot(all_heads, all_rows, preferred_element_type=jnp.float32)  9.08 us
    dot_general x4, matrix products, advance(): jnp.einsum('hid,hjd->hij', query_block, key_block, precision=HIGH) * lower  8.3 us
  transfers between devices with their start and end apart: 3, of which 3 were waited for; matrix products, arithmetic and copies ran while one was open for 16% of the time, Pallas kernels for 0%

commit v1 on v0

--- a/solution.py
+++ b/solution.py
@@ -81,7 +81,8 @@
     seq_count = lax.axis_size("seq")
     tok_count = length // head_count
     all_heads = lax.all_to_all(attn, "head", split_axis=0, concat_axis=1, tiled=True)
-    all_rows = lax.all_gather(out_weight, "head", axis=0, tiled=True)
+    repeated = jnp.stack([out_weight] * lax.axis_size("head"))
+    all_rows = jnp.concatenate(lax.all_to_all(repeated, "head", 0, 0), axis=0)
     projected = jnp.dot(all_heads, all_rows, preferred_element_type=jnp.float32)
     normed = (
         projected * lax.rsqrt(jnp.mean(projected * projected, axis=-1, keepdims=True) + 1e-06)

time: 278 us -> 474 us (1.71)
  waiting for transfers between devices: 69.9 us -> 248 us
  blocking collectives: 72.2 us -> 103 us
  between operations: 13.6 us -> 0.21 us
  local copies, waits for them, and re-layouts: 36.1 us -> 42.6 us
    all_to_all x1, waiting for transfers between devices: 9.66 us -> 195 us  [shards(): all_rows = jnp.concatenate(lax.all_to_all(repeated, 'head', 0, 0), axis=0)]
    all_to_all x0 -> x1, blocking collectives: none -> 21.8 us  [shards(): lax.all_to_all(attn, 'head', split_axis=0, concat_axis=1, tiled=True)]
    all_to_all x1, blocking collectives: 60.2 us -> 69.1 us  [exchange_both(): lax.all_to_all(blocks, axis, split_axis=0, concat_axis=0, tiled=True)]
    all_gather x1 -> x0, waiting for transfers between devices: 6.9 us -> none  [shards(): all_rows = lax.all_gather(out_weight, 'head', axis=0, tiled=True)]
    another operation x3 -> x4, local copies, waits for them, and re-layouts: 0.03 us -> 6.81 us  [the longest x1 6.78 us: shards(): repeated = jnp.stack([out_weight] * lax.axis_size('head'))]
  transfers between devices with their start and end apart: 3 -> 2, of which waited for: 3 -> 2; matrix products, arithmetic and copies ran while one was open for 16% -> 1% of each run, Pallas kernels for 0% -> 0%
where the time goes in v1:
time: 474 us; the launch traced here: 472 us
  waiting for transfers between devices  248 us (52%)
  blocking collectives  103 us (22%)
  matrix products  58.4 us (12%)
  local copies, waits for them, and re-layouts  42.6 us (9%)
  starting transfers between devices  10.9 us (2%)
  other arithmetic  9.54 us (2%)
    all_to_all x1, waiting for transfers between devices, shards(): all_rows = jnp.concatenate(lax.all_to_all(repeated, 'head', 0, 0), axis=0)  195 us
    all_to_all x1, blocking collectives, exchange_both(): lax.all_to_all(blocks, axis, split_axis=0, concat_axis=0, tiled=True)  69.1 us
    all_to_all x1, waiting for transfers between devices, exchange_both(): lax.all_to_all(blocks, axis, split_axis=0, concat_axis=0, tiled=True)  52.6 us
    all_to_all x1, blocking collectives, shards(): lax.all_to_all(attn, 'head', split_axis=0, concat_axis=1, tiled=True)  21.8 us
    dot_general x1, matrix products, shards(): jnp.einsum('nesf,efd->nesd', act, w_down, preferred_element_type=jnp.floa...  12.3 us
    all_gather x1, blocking collectives, shards(): lax.all_gather(local_state[None].astype(jnp.bfloat16), 'seq', axis=0, til...  11.6 us
  transfers between devices with their start and end apart: 2, of which 2 were waited for; matrix products, arithmetic and copies ran while one was open for 1% of the time, Pallas kernels for 0%

profile of v1, /device:TPU:1, one launch (start us, length us, event | category | flops | bytes accessed | tf_op | source)
XLA Modules:
  0.0 472.3 jit_solution(7150347223014566401)
XLA Ops:
  0.0 30.8 %while.13 = (s32[]{:T(128)}, f32[1,128,128]{2,1,0:T(8,128)S(1)}, f32[4,1,512,128]{3,2,1,0:T(8,128)}, f32[4,1,512,128]{3,2,1,0:T(8,128)}, f32[4,1,512,128]{3,2,1,...) while((s32[]{:T(128)}, f32[1,128,128]{2,1,0:T(8,128)S(1)}, ...), condition=%wide.region_1.2_spmd.clone, body=%wide.region_0.1_spmd.clone.sunk | while | flops 1007534080 | bytes 4657258 | solution.py:53
  0.0 2.2 convolution_multiply_fusion.2
  4.1 2.0 fusion.87
  7.8 2.0 convolution_multiply_fusion.2
  11.8 2.0 fusion.87
  15.5 2.0 convolution_multiply_fusion.2
  19.4 2.0 fusion.87
  23.1 2.0 convolution_multiply_fusion.2
  27.1 2.0 fusion.87
  30.8 2.6 copy.36
  33.4 11.6 %all-gather = bf16[4,128,128]{2,1,0:T(8,128)(2,1)S(1)} all-gather(bf16[1,128,128]{2,1,0:T(8,128)(2,1)S(1)} %convert_element_type.66), channel_id=2, replica_groups=mesh['seq'=4,'head'=32] {'seq'}, dimensions={0}, use_global_device_ids=true | all-gather | bytes 163840 | tf_op jit(solution)/shard_map/all_gather | solution.py:68
  45.1 2.7 multiply_reduce_fusion
  48.6 2.0 copy.26
  50.6 21.8 %all_to_all.28 = bf16[32,64,128]{2,1,0:T(8,128)(2,1)} all-to-all(bf16[32,64,128]{2,1,0:T(8,128)(2,1)} %bitcast.179), channel_id=1, replica_groups=mesh['seq'=4,'head'=32] {'head'}, dimensions={0} | all-to-all | bytes 1048576 | tf_op jit(solution)/shard_map/all_to_all | solution.py:83
  72.5 6.8 %stack.2 = bf16[32,128,2048]{2,1,0:T(8,128)(2,1)} broadcast(bf16[128,2048]{1,0:T(8,128)(2,1)} %param.14), dimensions={1,2} | broadcast | bytes 17301504 | tf_op jit(solution)/shard_map/stack | solution.py:84
  79.3 5.3 %all-to-all-start.1 = ((bf16[32,128,2048]{2,1,0:T(8,128)(2,1)}), bf16[32,128,2048]{2,1,0:T(8,128)(2,1)}, u32[]{:S(2)}, u32[]{:S(2)}) async-start(bf16[32,128,2048]{2,1,0:T(8,128)(2,1)} %stack.2), calls=%async_computation.1 | async-start | bytes 33554432 | tf_op jit(solution)/shard_map/all_to_all | solution.py:85
  85.8 2.4 scatter_custom_fusion.1
  88.2 2.4 scatter_custom_fusion
  90.8 195.3 %all-to-all-done.1 = bf16[32,128,2048]{2,1,0:T(8,128)(2,1)} async-done(((bf16[32,128,2048]{2,1,0:T(8,128)(2,1)}), bf16[32,128,2048]{2,1,0:T(8,128)(2,1)}, u32[]{:S(2)}, u32[]{:S(2)}) %all-to-all-start.1) | async-done | bytes 16777248 | tf_op jit(solution)/shard_map/all_to_all | solution.py:85
  286.1 7.6 %multiply_reduce_fusion.1 = (f32[64]{0:T(128)S(1)}, f32[64,2048]{1,0:T(8,128)S(1)}) fusion(bf16[32,128,2048]{2,1,0:T(8,128)(2,1)} %all-to-all-done.1, bf16[32,64,128]{2,1,0:T(8,128)(2,1)} %all_to_all.28), kind=kOutput, calls=%fused_computation.58 | convolution fusion | flops 1074003968 | bytes 17826048 | tf_op jit(solution)/shard_map/dot_general | solution.py:86
  294.6 6.0 %gather_fusion = bf16[1024,2048]{1,0:T(8,128)(2,1)} fusion(bf16[64,2048]{1,0:T(8,128)(2,1)S(1)} %multiply_convert_fusion.1, s32[1024]{0:T(1024)S(1)} %fusion.53), kind=kCustom, calls=%fused_computation | custom fusion | bytes 8392704 | tf_op jit(solution)/shard_map/gather | solution.py:110
  300.7 2.5 bitcast_select_fusion
  303.2 69.1 %all_to_all.29 = bf16[128,1,1,1,8,2048]{5,4,3,2,1,0:T(8,128)(2,1)S(1)} all-to-all(bf16[128,1,1,1,8,2048]{5,4,3,2,1,0:T(8,128)(2,1)S(1)} %bitcast_select_fusion), channel_id=1, replica_groups=mesh['seq'=4,'head'=32] {'seq','head'}, dimensions={0} | all-to-all | bytes 8388608 | tf_op jit(solution)/shard_map/all_to_all | solution.py:29
  372.3 2.3 copy.33
  374.7 2.0 copy-done.2
  376.6 5.2 %fusion.30 = f32[128,8,768]{2,0,1:T(8,128)} fusion(bf16[128,8,2048]{2,0,1:T(8,128)(2,1)S(1)} %bitcast.177, bf16[1,2048,768]{2,1,0:T(8,128)(2,1)S(1)} %copy-done.5), kind=kOutput, calls=%fused_computation.41 | convolution fusion | flops 3221225472 | bytes 10485760 | tf_op jit(solution)/shard_map/nesd,edf->nesf/dot_general | solution.py:118
  381.8 12.3 %convert_bitcast_fusion = bf16[128,1,1,1,8,2048]{5,0,4,3,2,1:T(8,128)(2,1)} fusion(bf16[1,768,2048]{2,1,0:T(8,128)(2,1)S(1)} %copy-done, f32[128,8,768]{2,0,1:T(8,128)} %fusion.30, bf16[128,8,2048]{2,0,1:T(8,128)(2,1)} %bitcast.178, bf16[1,2048,768]{2,1,0:T(8,128)(2,1)} %param.17), kind=kOutput, calls=%fused_computation.37 | convolution fusion | flops 6449266688 | bytes 17825792 | tf_op jit(solution)/shard_map/nesf,efd->nesd/dot_general | solution.py:120
  394.1 6.5 %copy.34 = bf16[128,1,1,1,8,2048]{5,4,3,2,1,0:T(8,128)(2,1)} copy(bf16[128,1,1,1,8,2048]{5,0,4,3,2,1:T(8,128)(2,1)} %convert_bitcast_fusion) | data formatting | bytes 8388608 | tf_op jit(solution)/shard_map/reshape;transpose;transpose;reshape;reshape;reshape | solution.py:28
  400.6 5.6 %all-to-all-start.3 = ((bf16[128,1,1,1,8,2048]{5,4,3,2,1,0:T(8,128)(2,1)}), bf16[128,1,1,1,8,2048]{5,4,3,2,1,0:T(8,128)(2,1)}, u32[]{:S(2)}, u32[]{:S(2)}) async-start(bf16[128,1,1,1,8,2048]{5,4,3,2,1,0:T(8,128)(2,1)} %copy.34), calls=%async_computation.3 | async-start | bytes 8388608 | tf_op jit(solution)/shard_map/all_to_all | solution.py:29
  406.3 52.6 %all-to-all-done.3 = bf16[128,1,1,1,8,2048]{5,4,3,2,1,0:T(8,128)(2,1)} async-done(((bf16[128,1,1,1,8,2048]{5,4,3,2,1,0:T(8,128)(2,1)}), bf16[128,1,1,1,8,2048]{5,4,3,2,1,0:T(8,128)(2,1)}, u32[]{:S(2)}, u32[]{:S(2)}) %all-to-all-start.3) | async-done | bytes 4194336 | tf_op jit(solution)/shard_map/all_to_all | solution.py:29
  459.0 8.0 %gather_fusion.1 = bf16[512,2048]{1,0:T(8,128)(2,1)} fusion(bf16[1024,2048]{1,0:T(8,128)(2,1)} %bitcast.47, s32[1024]{0:T(1024)S(1)} %pad_clamp_fusion), kind=kCustom, calls=%fused_computation.1 | custom fusion | bytes 4196352 | tf_op jit(solution)/shard_map/gather | solution.py:126
  467.0 3.4 fusion.27
  (53 shorter events, 19.4 us)
Async XLA Ops:
  0.0 381.8 %copy-start = (bf16[1,768,2048]{2,1,0:T(8,128)(2,1)S(1)}, bf16[1,768,2048]{2,1,0:T(8,128)(2,1)}, u32[]{:S(2)}) copy-start(bf16[1,768,2048]{2,1,0:T(8,128)(2,1)} %param.19) | copy-start | bytes 9437188
  79.3 5.3 %copy-start.3 = (s32[64,8]{0,1:T(8,128)S(1)}, s32[64,8]{0,1:T(8,128)}, u32[]{:S(2)}) copy-start(s32[64,8]{0,1:T(8,128)} %param.15) | copy-start | bytes 6148
  79.3 206.8 %all-to-all-start.1 = ((bf16[32,128,2048]{2,1,0:T(8,128)(2,1)}), bf16[32,128,2048]{2,1,0:T(8,128)(2,1)}, u32[]{:S(2)}, u32[]{:S(2)}) async-start(bf16[32,128,2048]{2,1,0:T(8,128)(2,1)} %stack.2), calls=%async_computation.1 | async-start | bytes 33554432 | tf_op jit(solution)/shard_map/all_to_all | solution.py:85
  293.7 0.8 copy-start.1
  372.3 4.3 copy-start.5
  374.6 2.0 copy-start.2
  400.6 5.6 %copy-start.4 = (s32[64,8]{0,1:T(8,128)S(1)}, s32[64,8]{0,1:T(8,128)}, u32[]{:S(2)}) copy-start(s32[64,8]{0,1:T(8,128)} %param.16) | copy-start | bytes 6148
  400.6 58.4 %all-to-all-start.3 = ((bf16[128,1,1,1,8,2048]{5,4,3,2,1,0:T(8,128)(2,1)}), bf16[128,1,1,1,8,2048]{5,4,3,2,1,0:T(8,128)(2,1)}, u32[]{:S(2)}, u32[]{:S(2)}) async-start(bf16[128,1,1,1,8,2048]{5,4,3,2,1,0:T(8,128)(2,1)} %copy.34), calls=%async_computation.3 | async-start | bytes 8388608 | tf_op jit(solution)/shard_map/all_to_all | solution.py:29
